TPU v7x, 512 devices: a whole 4x8x8 slice. The times are simulated.
512 devices in a mesh: grp: 2 (over core), kv: 8 (over z), srv: 32 (over x, y).
Axes of the slice: x: 4, y: 8, z: 8, core: 2. Of those that a mesh axis runs over, the one named last changes fastest.
Arguments:
- queries: bfloat16 [8192, 8, 1024], P('srv', 'kv', 'grp'), may hold values from -120 to 120
- keys: bfloat16 [8192, 8, 128], P('srv', 'kv'), may hold values from -5 to 5
- values: bfloat16 [8192, 8, 128], P('srv', 'kv'), may hold values from -6 to 6
- lengths: int32 [16], replicated, may hold values from 1 to 1024, 8192 in all
- output_projection_weight: bfloat16 [8, 1024, 8192], P('kv', 'grp', 'srv'), may hold values from -0.0625 to 0.0625
Outputs:
- projected: bfloat16 [8192, 8192], P('srv', ('grp', 'kv'))
Inputs may be any that keep to these rules, and one draw needn't show every extreme that they name: The 16 lengths sum to 8192; the longest document has exactly 1024 tokens.
All inputs are finite; a program needn't handle non-finite values.
Results may differ from a plain program's by a relative error of at most 0.017.
Values may be sent and summed in bfloat16 or wider, within the bound.
No kernel may reach another device: no remote copies, remote signals or barrier semaphores. Data moves between devices by JAX's collectives and lax.ppermute only.
A program may use at most 64 MiB of HBM per device.

v0:
```python
import math
import jax
import jax.numpy as jnp
from jax import lax
from jax.sharding import PartitionSpec as P

REACH = 4


def from_behind(block, axis, distance):
    devices = range(lax.axis_size(axis))
    route = [(i - distance, i) for i in devices if i - distance in devices]
    return lax.ppermute(block, axis, route)


def sum_by_axis(array, axes, dim):
    if not axes:
        return array
    nearer = lax.psum_scatter(array, axes[0], scatter_dimension=dim, tiled=True)
    return sum_by_axis(nearer, axes[1:], dim)


def doc_starts(lengths, position):
    starts = jnp.cumsum(lengths) - lengths
    chosen = jnp.where(starts[None, :] <= position[:, None], starts[None, :], 0)
    return jnp.max(chosen, axis=1)


def attend(queries, window_keys, window_values, query_pos, key_pos, lengths):
    token_count = queries.shape[0]
    groups = queries.shape[1]
    head_size = window_keys.shape[2]
    heads = queries.shape[2] // head_size
    split_output = queries.reshape(token_count, groups, heads, head_size)
    scores = jnp.einsum(
        "tjhd,wjd->jhtw", split_output, window_keys, preferred_element_type=jnp.float32
    )
    scores = scores * (1.0 / math.sqrt(head_size))
    first_key = doc_starts(lengths, query_pos)
    allowed = (key_pos[None, :] >= first_key[:, None]) & (key_pos[None, :] <= query_pos[:, None])
    scores = jnp.where(allowed[None, None], scores, -jnp.inf)
    peak = jnp.max(scores, axis=3, keepdims=True)
    weights = jnp.exp(scores - peak)
    total = jnp.sum(weights, axis=3)
    numer = jnp.einsum(
        "jhtw,wjd->tjhd",
        weights.astype(jnp.bfloat16),
        window_values,
        preferred_element_type=jnp.float32,
    )
    final_output = numer / jnp.transpose(total, (2, 0, 1))[..., None]
    return final_output.astype(jnp.bfloat16).reshape(token_count, groups * heads * head_size)


def on_device(queries, keys, values, lengths, output_projection_weight):
    token_count = queries.shape[0]
    shard = lax.axis_index("srv")
    stacked = jnp.stack([keys, values])
    arrived = [stacked]
    for distance in range(1, REACH + 1):
        arrived.append(from_behind(stacked, "srv", distance))
    window = jnp.concatenate(arrived[::-1], axis=1)
    query_pos = shard * token_count + jnp.arange(token_count, dtype=jnp.int32)
    key_pos = (shard - REACH) * token_count + jnp.arange(window.shape[1], dtype=jnp.int32)
    attention_output = attend(queries, window[0], window[1], query_pos, key_pos, lengths)
    inner = attention_output.shape[1]
    piece = lax.all_gather(output_projection_weight, "srv", axis=2, tiled=True)
    partial_sum = jnp.dot(
        attention_output, piece.reshape(inner, piece.shape[2]), preferred_element_type=jnp.float32
    )
    summed = sum_by_axis(partial_sum.astype(jnp.bfloat16), ("grp", "kv"), 1).astype(jnp.float32)
    return summed.astype(jnp.bfloat16)


def solution(mesh):
    placed = (
        P("srv", "kv", "grp"),
        P("srv", "kv", None),
        P("srv", "kv", None),
        P(),
        P("kv", "grp", "srv"),
    )
    return jax.shard_map(
        on_device, mesh=mesh, in_specs=placed, out_specs=P("srv", ("grp", "kv")), check_vma=False
    )
```

profile of v0, /device:TPU:4, one launch (start us, length us, event | category | flops | bytes accessed | tf_op | source)
XLA Modules:
  0.0 212.5 jit_solution(3647171846262931791)
XLA Ops:
  6.5 0.7 all-gather.2.cloned.1.call-update
  7.3 0.9 pad_maximum_fusion
  8.2 7.7 %collective-permute-start = (bf16[2,256,1,128]{3,1,2,0:T(8,128)(2,1)S(1)}, bf16[2,256,1,128]{3,1,2,0:T(8,128)(2,1)S(1)}, u32[]{:S(2)}, u32[]{:S(2)}) collective-permute-start(bf16[2,256,1,128]{3,1,2,0:T(8,128)(2,1)S(1)} %pad_maximum_fusion), channel_id=1, source_target_pairs={{0,4},{1,5},{2,6},{3,7},{4,8},{5,9},{6,10},{7,11},{8,12},{9,13},{1... | collective-permute-start | bytes 393224 | tf_op jit(solution)/shard_map/ppermute | solution.py:13
  15.9 2.8 %collective-permute-start.1 = (bf16[2,256,1,128]{3,1,2,0:T(8,128)(2,1)S(1)}, bf16[2,256,1,128]{3,1,2,0:T(8,128)(2,1)S(1)}, u32[]{:S(2)}, u32[]{:S(2)}) collective-permute-start(bf16[2,256,1,128]{3,1,2,0:T(8,128)(2,1)S(1)} %pad_maximum_fusion), channel_id=1, source_target_pairs={{0,3},{1,4},{2,5},{3,6},{4,7},{5,8},{6,9},{7,10},{8,11},{9,12},{10... | collective-permute-start | bytes 393224 | tf_op jit(solution)/shard_map/ppermute | solution.py:13
  18.8 3.3 %collective-permute-start.2 = (bf16[2,256,1,128]{3,1,2,0:T(8,128)(2,1)S(1)}, bf16[2,256,1,128]{3,1,2,0:T(8,128)(2,1)S(1)}, u32[]{:S(2)}, u32[]{:S(2)}) collective-permute-start(bf16[2,256,1,128]{3,1,2,0:T(8,128)(2,1)S(1)} %pad_maximum_fusion), channel_id=1, source_target_pairs={{0,2},{1,3},{2,4},{3,5},{4,6},{5,7},{6,8},{7,9},{8,10},{9,11},{10,... | collective-permute-start | bytes 393224 | tf_op jit(solution)/shard_map/ppermute | solution.py:13
  22.1 3.5 %collective-permute-start.3 = (bf16[2,256,1,128]{3,1,2,0:T(8,128)(2,1)S(1)}, bf16[2,256,1,128]{3,1,2,0:T(8,128)(2,1)S(1)}, u32[]{:S(2)}, u32[]{:S(2)}) collective-permute-start(bf16[2,256,1,128]{3,1,2,0:T(8,128)(2,1)S(1)} %pad_maximum_fusion), channel_id=1, source_target_pairs={{0,1},{1,2},{2,3},{3,4},{4,5},{5,6},{6,7},{7,8},{8,9},{9,10},{10,1... | collective-permute-start | bytes 393224 | tf_op jit(solution)/shard_map/ppermute | solution.py:13
  25.6 0.7 copy.14
  26.4 0.1 reduce.2
  26.5 0.7 sub.15
  27.1 0.1 select_reduce_fusion
  27.2 0.3 compare_and_fusion
  27.6 1.0 reshape.130
  28.6 5.6 %collective-permute-done.1 = bf16[2,256,1,128]{3,1,2,0:T(8,128)(2,1)S(1)} collective-permute-done((bf16[2,256,1,128]{3,1,2,0:T(8,128)(2,1)S(1)}, bf16[2,256,1,128]{3,1,2,0:T(8,128)(2,1)S(1)}, u32[]{:S(2)}, u32[]{:S(2)}) %collective-permute-start.1) | collective-permute-done | bytes 131104 | tf_op jit(solution)/shard_map/ppermute | solution.py:13
  34.2 1.8 collective-permute-done.2
  36.1 5.3 %collective-permute-done.3 = bf16[2,256,1,128]{3,1,2,0:T(8,128)(2,1)S(1)} collective-permute-done((bf16[2,256,1,128]{3,1,2,0:T(8,128)(2,1)S(1)}, bf16[2,256,1,128]{3,1,2,0:T(8,128)(2,1)S(1)}, u32[]{:S(2)}, u32[]{:S(2)}) %collective-permute-start.3) | collective-permute-done | bytes 131104 | tf_op jit(solution)/shard_map/ppermute | solution.py:13
  41.4 0.9 constant_dynamic-update-slice_fusion
  42.3 1.0 fusion.17
  43.3 0.7 fusion.1
  44.0 1.0 fusion.13
  45.0 83.4 %all-gather.2.cloned.1.call-done = bf16[1,512,8192]{2,1,0:T(8,128)(2,1)} async-done(((bf16[1,512,256]{2,1,0:T(8,128)(2,1)}), bf16[1,512,8192]{2,1,0:T(8,128)(2,1)}) %all-gather.2.cloned.1.call-update) | async-done | bytes 8388624 | tf_op jit(solution)/shard_map/all_gather | solution.py:67
  128.4 7.7 %convolution_convert_fusion = bf16[256,8192]{1,0:T(8,128)(2,1)} fusion(bf16[256,512]{0,1:T(8,128)(2,1)S(1)} %bitcast.48, bf16[1,512,8192]{2,1,0:T(8,128)(2,1)} %all-gather.2.cloned.1.call-done), kind=kOutput, calls=%fused_computation | convolution fusion | flops 2149580800 | bytes 12845056 | tf_op jit(solution)/shard_map/dot_general | solution.py:68
  136.1 0.0 reduce-scatter.5.cloned.1.call-start
  136.2 19.5 %reduce-scatter.3.cloned.1.call-done = bf16[256,4096]{1,0:T(8,128)(2,1)} async-done(((bf16[256,8192]{1,0:T(8,128)(2,1)}), bf16[256,4096]{1,0:T(8,128)(2,1)}) %reduce-scatter.3.cloned.1.call-update) | async-done | bytes 2097168 | tf_op jit(solution)/shard_map/reduce_scatter | solution.py:19
  155.7 50.3 %reduce-scatter.5.cloned.1.call-done = bf16[256,512]{1,0:T(8,128)(2,1)} async-done(((bf16[256,4096]{1,0:T(8,128)(2,1)}), bf16[256,512]{1,0:T(8,128)(2,1)}) %reduce-scatter.5.cloned.1.call-update) | async-done | bytes 262160 | tf_op jit(solution)/shard_map/reduce_scatter | solution.py:19
  (12 shorter events, 0.2 us)
Async XLA Ops:
  6.5 121.9 %all-gather.2.cloned.1.call-start = ((), (), s32[]{:S(2)}) async-start(), calls=%async_computation.2 | async-start | bytes 8650752 | tf_op jit(solution)/shard_map/all_gather | solution.py:67
  7.3 148.4 %reduce-scatter.3.cloned.1.call-start = ((), (), s32[]{:S(2)}) async-start(), calls=%async_computation.3 | async-start | bytes 6291456 | tf_op jit(solution)/shard_map/reduce_scatter | solution.py:19
  8.2 20.4 %collective-permute-start = (bf16[2,256,1,128]{3,1,2,0:T(8,128)(2,1)S(1)}, bf16[2,256,1,128]{3,1,2,0:T(8,128)(2,1)S(1)}, u32[]{:S(2)}, u32[]{:S(2)}) collective-permute-start(bf16[2,256,1,128]{3,1,2,0:T(8,128)(2,1)S(1)} %pad_maximum_fusion), channel_id=1, source_target_pairs={{0,4},{1,5},{2,6},{3,7},{4,8},{5,9},{6,10},{7,11},{8,12},{9,13},{1... | collective-permute-start | bytes 393224 | tf_op jit(solution)/shard_map/ppermute | solution.py:13
  15.9 18.3 %collective-permute-start.1 = (bf16[2,256,1,128]{3,1,2,0:T(8,128)(2,1)S(1)}, bf16[2,256,1,128]{3,1,2,0:T(8,128)(2,1)S(1)}, u32[]{:S(2)}, u32[]{:S(2)}) collective-permute-start(bf16[2,256,1,128]{3,1,2,0:T(8,128)(2,1)S(1)} %pad_maximum_fusion), channel_id=1, source_target_pairs={{0,3},{1,4},{2,5},{3,6},{4,7},{5,8},{6,9},{7,10},{8,11},{9,12},{10... | collective-permute-start | bytes 393224 | tf_op jit(solution)/shard_map/ppermute | solution.py:13
  18.8 17.3 %collective-permute-start.2 = (bf16[2,256,1,128]{3,1,2,0:T(8,128)(2,1)S(1)}, bf16[2,256,1,128]{3,1,2,0:T(8,128)(2,1)S(1)}, u32[]{:S(2)}, u32[]{:S(2)}) collective-permute-start(bf16[2,256,1,128]{3,1,2,0:T(8,128)(2,1)S(1)} %pad_maximum_fusion), channel_id=1, source_target_pairs={{0,2},{1,3},{2,4},{3,5},{4,6},{5,7},{6,8},{7,9},{8,10},{9,11},{10,... | collective-permute-start | bytes 393224 | tf_op jit(solution)/shard_map/ppermute | solution.py:13
  22.1 19.3 %collective-permute-start.3 = (bf16[2,256,1,128]{3,1,2,0:T(8,128)(2,1)S(1)}, bf16[2,256,1,128]{3,1,2,0:T(8,128)(2,1)S(1)}, u32[]{:S(2)}, u32[]{:S(2)}) collective-permute-start(bf16[2,256,1,128]{3,1,2,0:T(8,128)(2,1)S(1)} %pad_maximum_fusion), channel_id=1, source_target_pairs={{0,1},{1,2},{2,3},{3,4},{4,5},{5,6},{6,7},{7,8},{8,9},{9,10},{10,1... | collective-permute-start | bytes 393224 | tf_op jit(solution)/shard_map/ppermute | solution.py:13
  136.1 69.8 %reduce-scatter.5.cloned.1.call-start = ((), (), s32[]{:S(2)}) async-start(), calls=%async_computation.4 | async-start | bytes 2359296 | tf_op jit(solution)/shard_map/reduce_scatter | solution.py:19
Sparse Core Ops, SparseCore 0:
  10.4 117.9 all-gather.1
  136.3 19.3 reduce-scatter.2
  158.8 47.1 reduce-scatter.4
where the time goes:
time: 213 us; the launch traced here: 212 us
  waiting for transfers between devices  167 us (78%)
  starting transfers between devices  17.4 us (8%)
  between operations  13.2 us (6%)
  matrix products  9.7 us (5%)
  other arithmetic  3.71 us (2%)
    all_gather x1, waiting for transfers between devices, on_device(): piece = lax.all_gather(output_projection_weight, 'srv', axis=2, tiled=True)  83.4 us
    reduce_scatter x2, waiting for transfers between devices, sum_by_axis(): nearer = lax.psum_scatter(array, axes[0], scatter_dimension=dim, tiled=True)  69.7 us
    ppermute x4, starting transfers between devices, from_behind(): return lax.ppermute(block, axis, route)  17.4 us
    ppermute x4, waiting for transfers between devices, from_behind(): return lax.ppermute(block, axis, route)  12.7 us
    dot_general x1, matrix products, on_device(): jnp.dot(attention_output, piece.reshape(inner, piece.shape[2]), preferred...  7.73 us
  transfers between devices with their start and end apart: 7, of which 6 were waited for; matrix products, arithmetic and copies ran while one was open for 4% of the time, Pallas kernels for 0%

commit v1 on v0

--- a/solution.py
+++ b/solution.py
@@ -64,7 +64,10 @@
     key_pos = (shard - REACH) * token_count + jnp.arange(window.shape[1], dtype=jnp.int32)
     attention_output = attend(queries, window[0], window[1], query_pos, key_pos, lengths)
     inner = attention_output.shape[1]
-    piece = lax.all_gather(output_projection_weight, "srv", axis=2, tiled=True)
+    piece = jnp.concatenate(
+        lax.all_to_all(jnp.stack([output_projection_weight] * lax.axis_size("srv")), "srv", 0, 0),
+        axis=2,
+    )
     partial_sum = jnp.dot(
         attention_output, piece.reshape(inner, piece.shape[2]), preferred_element_type=jnp.float32
     )

time: 213 us -> 326 us (1.53)
  the two profiles are of different devices: /device:TPU:4 before, /device:TPU:6 now
where the time goes in v1:
time: 326 us
  waiting for transfers between devices  271 us (83%)
  starting transfers between devices  25 us (8%)
  between operations  13.6 us (4%)
  matrix products  9.76 us (3%)
  local copies, waits for them, and re-layouts  5.48 us (2%)
    ppermute x4, waiting for transfers between devices, from_behind(): return lax.ppermute(block, axis, route)  199 us
    reduce_scatter x2, waiting for transfers between devices, sum_by_axis(): nearer = lax.psum_scatter(array, axes[0], scatter_dimension=dim, tiled=True)  72.2 us
    ppermute x4, starting transfers between devices, from_behind(): return lax.ppermute(block, axis, route)  14.2 us
    all_to_all x1, starting transfers between devices, on_device(): lax.all_to_all(jnp.stack([output_projection_weight] * lax.axis_size('srv'...  10.7 us
    dot_general x1, matrix products, on_device(): jnp.dot(attention_output, piece.reshape(inner, piece.shape[2]), preferred...  7.77 us
  transfers between devices with their start and end apart: 7, of which 3 were waited for; matrix products, arithmetic and copies ran while one was open for 1% of the time, Pallas kernels for 0%

profile of v1, /device:TPU:6, one launch (start us, length us, event | category | flops | bytes accessed | tf_op | source)
XLA Modules:
  0.0 326.2 jit_solution(6398187930511812252)
XLA Ops:
  6.5 1.1 copy.25
  7.6 4.2 %stack.11 = bf16[32,1,512,256]{2,3,1,0:T(8,128)(2,1)} broadcast(bf16[512,256]{0,1:T(8,128)(2,1)S(1)} %copy.25), dimensions={2,3} | broadcast | bytes 8650752 | tf_op jit(solution)/shard_map/stack | solution.py:68
  11.8 10.7 %all-to-all-start = ((bf16[32,1,512,256]{2,3,1,0:T(8,128)(2,1)}), bf16[32,1,512,256]{2,3,1,0:T(8,128)(2,1)}, u32[]{:S(2)}, u32[]{:S(2)}) async-start(bf16[32,1,512,256]{2,3,1,0:T(8,128)(2,1)} %stack.11), calls=%async_computation | async-start | bytes 16777216 | tf_op jit(solution)/shard_map/all_to_all | solution.py:68
  22.5 0.0 reduce-scatter.3.cloned.1.call-start
  22.6 3.4 %collective-permute-start.3 = (bf16[2,256,1,128]{3,1,2,0:T(8,128)(2,1)S(1)}, bf16[2,256,1,128]{3,1,2,0:T(8,128)(2,1)S(1)}, u32[]{:S(2)}, u32[]{:S(2)}) collective-permute-start(bf16[2,256,1,128]{3,1,2,0:T(8,128)(2,1)S(1)} %pad_maximum_fusion), channel_id=1, source_target_pairs={{0,1},{1,2},{2,3},{3,4},{4,5},{5,6},{6,7},{7,8},{8,9},{9,10},{10,1... | collective-permute-start | bytes 393224 | tf_op jit(solution)/shard_map/ppermute | solution.py:13
  26.0 4.3 %collective-permute-start.2 = (bf16[2,256,1,128]{3,1,2,0:T(8,128)(2,1)S(1)}, bf16[2,256,1,128]{3,1,2,0:T(8,128)(2,1)S(1)}, u32[]{:S(2)}, u32[]{:S(2)}) collective-permute-start(bf16[2,256,1,128]{3,1,2,0:T(8,128)(2,1)S(1)} %pad_maximum_fusion), channel_id=1, source_target_pairs={{0,2},{1,3},{2,4},{3,5},{4,6},{5,7},{6,8},{7,9},{8,10},{9,11},{10,... | collective-permute-start | bytes 393224 | tf_op jit(solution)/shard_map/ppermute | solution.py:13
  30.3 4.6 %collective-permute-start.1 = (bf16[2,256,1,128]{3,1,2,0:T(8,128)(2,1)S(1)}, bf16[2,256,1,128]{3,1,2,0:T(8,128)(2,1)S(1)}, u32[]{:S(2)}, u32[]{:S(2)}) collective-permute-start(bf16[2,256,1,128]{3,1,2,0:T(8,128)(2,1)S(1)} %pad_maximum_fusion), channel_id=1, source_target_pairs={{0,3},{1,4},{2,5},{3,6},{4,7},{5,8},{6,9},{7,10},{8,11},{9,12},{10... | collective-permute-start | bytes 393224 | tf_op jit(solution)/shard_map/ppermute | solution.py:13
  34.9 1.9 collective-permute-start
  36.8 0.1 copy.21
  36.9 0.1 reduce.2
  37.1 0.1 select_reduce_fusion
  37.2 0.3 compare_and_fusion
  37.5 0.1 reshape.133
  37.6 198.8 %collective-permute-done = bf16[2,256,1,128]{3,1,2,0:T(8,128)(2,1)S(1)} collective-permute-done((bf16[2,256,1,128]{3,1,2,0:T(8,128)(2,1)S(1)}, bf16[2,256,1,128]{3,1,2,0:T(8,128)(2,1)S(1)}, u32[]{:S(2)}, u32[]{:S(2)}) %collective-permute-start) | collective-permute-done | bytes 131104 | tf_op jit(solution)/shard_map/ppermute | solution.py:13
  236.4 0.0 collective-permute-done.1
  236.6 1.0 fusion.16
  237.5 0.7 fusion
  238.2 1.0 fusion.12
  239.3 7.8 %convolution_convert_fusion = bf16[256,8192]{1,0:T(8,128)(2,1)} fusion(bf16[256,512]{0,1:T(8,128)(2,1)S(1)} %bitcast.52, bf16[512,8192]{0,1:T(8,128)(2,1)} %bitcast.19), kind=kOutput, calls=%fused_computation | convolution fusion | flops 2149580800 | bytes 12845056 | tf_op jit(solution)/shard_map/dot_general | solution.py:71
  247.1 0.0 reduce-scatter.3.cloned.1.call-update
  247.1 0.0 reduce-scatter.5.cloned.1.call-start
  247.1 21.9 %reduce-scatter.3.cloned.1.call-done = bf16[256,4096]{1,0:T(8,128)(2,1)} async-done(((bf16[256,8192]{1,0:T(8,128)(2,1)}), bf16[256,4096]{1,0:T(8,128)(2,1)}) %reduce-scatter.3.cloned.1.call-update) | async-done | bytes 2097168 | tf_op jit(solution)/shard_map/reduce_scatter | solution.py:19
  269.1 0.0 reduce-scatter.5.cloned.1.call-update
  269.1 50.2 %reduce-scatter.5.cloned.1.call-done = bf16[256,512]{1,0:T(8,128)(2,1)} async-done(((bf16[256,4096]{1,0:T(8,128)(2,1)}), bf16[256,512]{1,0:T(8,128)(2,1)}) %reduce-scatter.5.cloned.1.call-update) | async-done | bytes 262160 | tf_op jit(solution)/shard_map/reduce_scatter | solution.py:19
  (21 shorter events, 0.2 us)
Async XLA Ops:
  11.8 10.8 %copy-start.1 = (bf16[256,1,128]{2,0,1:T(8,128)(2,1)S(1)}, bf16[256,1,128]{2,0,1:T(8,128)(2,1)}, u32[]{:S(2)}) copy-start(bf16[256,1,128]{2,0,1:T(8,128)(2,1)} %param.7) | copy-start | bytes 196612
  11.8 10.8 %copy-start.2 = (bf16[256,1,128]{2,0,1:T(8,128)(2,1)S(1)}, bf16[256,1,128]{2,0,1:T(8,128)(2,1)}, u32[]{:S(2)}) copy-start(bf16[256,1,128]{2,0,1:T(8,128)(2,1)} %param.6) | copy-start | bytes 196612
  11.8 25.0 %copy-start.3 = (s32[16]{0:T(128)S(1)}, s32[16]{0:T(128)}, u32[]{:S(2)}) copy-start(s32[16]{0:T(128)} %param.8) | copy-start | bytes 196
  11.8 25.7 %copy-start = (bf16[256,1,512]{2,0,1:T(8,128)(2,1)S(1)}, bf16[256,1,512]{2,0,1:T(8,128)(2,1)}, u32[]{:S(2)}) copy-start(bf16[256,1,512]{2,0,1:T(8,128)(2,1)} %param.5) | copy-start | bytes 786436
  11.8 227.5 %all-to-all-start = ((bf16[32,1,512,256]{2,3,1,0:T(8,128)(2,1)}), bf16[32,1,512,256]{2,3,1,0:T(8,128)(2,1)}, u32[]{:S(2)}, u32[]{:S(2)}) async-start(bf16[32,1,512,256]{2,3,1,0:T(8,128)(2,1)} %stack.11), calls=%async_computation | async-start | bytes 16777216 | tf_op jit(solution)/shard_map/all_to_all | solution.py:68
  22.5 246.6 %reduce-scatter.3.cloned.1.call-start = ((), (), s32[]{:S(2)}) async-start(), calls=%async_computation.3 | async-start | bytes 6291456 | tf_op jit(solution)/shard_map/reduce_scatter | solution.py:19
  22.6 213.9 %collective-permute-start.3 = (bf16[2,256,1,128]{3,1,2,0:T(8,128)(2,1)S(1)}, bf16[2,256,1,128]{3,1,2,0:T(8,128)(2,1)S(1)}, u32[]{:S(2)}, u32[]{:S(2)}) collective-permute-start(bf16[2,256,1,128]{3,1,2,0:T(8,128)(2,1)S(1)} %pad_maximum_fusion), channel_id=1, source_target_pairs={{0,1},{1,2},{2,3},{3,4},{4,5},{5,6},{6,7},{7,8},{8,9},{9,10},{10,1... | collective-permute-start | bytes 393224 | tf_op jit(solution)/shard_map/ppermute | solution.py:13
  26.0 210.5 %collective-permute-start.2 = (bf16[2,256,1,128]{3,1,2,0:T(8,128)(2,1)S(1)}, bf16[2,256,1,128]{3,1,2,0:T(8,128)(2,1)S(1)}, u32[]{:S(2)}, u32[]{:S(2)}) collective-permute-start(bf16[2,256,1,128]{3,1,2,0:T(8,128)(2,1)S(1)} %pad_maximum_fusion), channel_id=1, source_target_pairs={{0,2},{1,3},{2,4},{3,5},{4,6},{5,7},{6,8},{7,9},{8,10},{9,11},{10,... | collective-permute-start | bytes 393224 | tf_op jit(solution)/shard_map/ppermute | solution.py:13
  30.3 206.2 %collective-permute-start.1 = (bf16[2,256,1,128]{3,1,2,0:T(8,128)(2,1)S(1)}, bf16[2,256,1,128]{3,1,2,0:T(8,128)(2,1)S(1)}, u32[]{:S(2)}, u32[]{:S(2)}) collective-permute-start(bf16[2,256,1,128]{3,1,2,0:T(8,128)(2,1)S(1)} %pad_maximum_fusion), channel_id=1, source_target_pairs={{0,3},{1,4},{2,5},{3,6},{4,7},{5,8},{6,9},{7,10},{8,11},{9,12},{10... | collective-permute-start | bytes 393224 | tf_op jit(solution)/shard_map/ppermute | solution.py:13
  34.9 201.5 %collective-permute-start = (bf16[2,256,1,128]{3,1,2,0:T(8,128)(2,1)S(1)}, bf16[2,256,1,128]{3,1,2,0:T(8,128)(2,1)S(1)}, u32[]{:S(2)}, u32[]{:S(2)}) collective-permute-start(bf16[2,256,1,128]{3,1,2,0:T(8,128)(2,1)S(1)} %pad_maximum_fusion), channel_id=1, source_target_pairs={{0,4},{1,5},{2,6},{3,7},{4,8},{5,9},{6,10},{7,11},{8,12},{9,13},{1... | collective-permute-start | bytes 393224 | tf_op jit(solution)/shard_map/ppermute | solution.py:13
  247.1 72.2 %reduce-scatter.5.cloned.1.call-start = ((), (), s32[]{:S(2)}) async-start(), calls=%async_computation.4 | async-start | bytes 2359296 | tf_op jit(solution)/shard_map/reduce_scatter | solution.py:19
Sparse Core Ops, SparseCore 0:
  247.2 21.8 reduce-scatter.2
  272.2 47.1 reduce-scatter.4
